TPU v7x, 256 devices: a whole 4x4x8 slice. The times are simulated.
256 devices in a mesh: dp: 128 (over z, y, x), tensor: 2 (over core).
Axes of the slice: x: 4, y: 4, z: 8, core: 2. Of those that a mesh axis runs over, the one named last changes fastest.
Arguments:
- master: float32 [8, 1536, 5120], P(None, ('dp', 'tensor')), may hold values from -6 to 6
- moment_one: float32 [8, 1536, 5120], P(None, ('dp', 'tensor')), may hold values from -2 to 2
- moment_two: float32 [8, 1536, 5120], P(None, ('dp', 'tensor')), may hold values from 0.01 to 1
- grad: float32 [8, 5120, 1536], P(None, 'dp', 'tensor'), may hold values from -70 to 70
Outputs:
- new_master: float32 [8, 5120, 1536], P(None, 'dp', 'tensor')
- new_moment_one: float32 [8, 5120, 1536], P(None, 'dp', 'tensor')
- new_moment_two: float32 [8, 5120, 1536], P(None, 'dp', 'tensor')
All inputs are finite; a program needn't handle non-finite values.
Results may differ from a plain program's by a relative error of at most 0.0003.
Values sent between devices are 32-bit elements; how exact they have to be, the bound alone decides.
A program may use at most 64 MiB of HBM per device.

v0:
```python
import jax
import jax.numpy as jnp
from jax import lax
from jax.sharding import PartitionSpec as P

D = 5120
MOE_FF = 1536
MATS = 8


bias_first = 0.9999734386011124
bias_second = 0.994079470779666


def prepare(stored, owners):
    mats, rows, width = stored.shape
    block = width // owners
    split = stored.reshape(mats, rows, owners, block)
    grouped = jnp.transpose(split, (2, 0, 1, 3))
    return grouped.reshape(owners, 1, 1, mats * rows * block)


def finish(arrived, mats, rows, block):
    sources = arrived.shape[1] * arrived.shape[2]
    unpacked = arrived.reshape(sources, mats, rows, block)
    ordered = jnp.transpose(unpacked, (1, 3, 0, 2))
    return ordered.reshape(mats, block, sources * rows)


def local(master, moment_one, moment_two, grad):
    owners = lax.axis_size("dp")
    mats, rows, width = master.shape
    block = width // owners
    local_sum = jnp.sum(grad * grad)
    total = lax.psum(local_sum, ("dp", "tensor"))
    count = float(MATS * D * MOE_FF)
    scale = jnp.minimum(
        jnp.float32(1.0), 0.5 * jnp.sqrt(jnp.float32(count)) / (jnp.sqrt(total) + 1e-06)
    )
    weights = finish(
        lax.all_to_all(
            lax.all_to_all(prepare(master, owners), "dp", split_axis=0, concat_axis=1, tiled=True),
            "tensor",
            split_axis=1,
            concat_axis=2,
            tiled=True,
        ),
        mats,
        rows,
        block,
    )
    first = finish(
        lax.all_to_all(
            lax.all_to_all(
                prepare(moment_one, owners), "dp", split_axis=0, concat_axis=1, tiled=True
            ),
            "tensor",
            split_axis=1,
            concat_axis=2,
            tiled=True,
        ),
        mats,
        rows,
        block,
    )
    second = finish(
        lax.all_to_all(
            lax.all_to_all(
                prepare(moment_two, owners), "dp", split_axis=0, concat_axis=1, tiled=True
            ),
            "tensor",
            split_axis=1,
            concat_axis=2,
            tiled=True,
        ),
        mats,
        rows,
        block,
    )
    clipped = scale * grad
    new_first = 0.9 * first + 0.1 * clipped
    new_second = 0.95 * second + 0.05 * clipped * clipped
    update = new_first / bias_first / (jnp.sqrt(new_second / bias_second) + 1e-08)
    new_weights = weights * (1.0 - 0.05 * 0.1) - 0.05 * update
    return (new_weights, new_first, new_second)


def solution(mesh):
    placed = (
        P(None, ("dp", "tensor"), None),
        P(None, ("dp", "tensor"), None),
        P(None, ("dp", "tensor"), None),
        P(None, "dp", "tensor"),
    )
    return jax.shard_map(
        local,
        mesh=mesh,
        in_specs=placed,
        out_specs=(P(None, "dp", "tensor"), P(None, "dp", "tensor"), P(None, "dp", "tensor")),
        check_vma=False,
    )
```

profile of v0, /device:TPU:65, one launch (start us, length us, event | category | flops | bytes accessed | tf_op | source)
XLA Modules:
  0.0 241.4 jit_solution(1966707899867881165)
XLA Ops:
  0.6 3.6 %reshape.54 = f32[8,6,128,40]{3,2,0,1:T(8,128)S(1)} reshape(f32[8,6,5120]{2,0,1:T(8,128)} %param.4) | data formatting | bytes 1966080 | tf_op jit(solution)/shard_map/reshape | solution.py:18
  4.3 1.9 copy.36
  6.2 3.2 %copy.37 = f32[128,1,1,1920]{3,2,1,0:T(1,128)} copy(f32[128,1,1,1920]{0,3,2,1:T(8,128)} %bitcast.57) | data formatting | bytes 1966080 | tf_op jit(solution)/shard_map/reshape | solution.py:20
  9.4 14.5 %all-to-all-start = ((f32[128,1,1,1920]{3,2,1,0:T(1,128)}), f32[128,1,1,1920]{3,2,1,0:T(1,128)}, u32[]{:S(2)}, u32[]{:S(2)}) async-start(f32[128,1,1,1920]{3,2,1,0:T(1,128)} %copy.37), calls=%async_computation | async-start | bytes 1966080 | tf_op jit(solution)/shard_map/all_to_all | solution.py:42
  23.9 3.6 %reshape.56 = f32[8,6,128,40]{3,2,0,1:T(8,128)S(1)} reshape(f32[8,6,5120]{2,0,1:T(8,128)} %param.5) | data formatting | bytes 1966080 | tf_op jit(solution)/shard_map/reshape | solution.py:18
  27.5 1.9 copy.42
  29.4 3.2 %copy.43 = f32[128,1,1,1920]{3,2,1,0:T(1,128)} copy(f32[128,1,1,1920]{0,3,2,1:T(8,128)} %bitcast.58) | data formatting | bytes 1966080 | tf_op jit(solution)/shard_map/reshape | solution.py:20
  32.6 17.3 %all-to-all-done = f32[128,1,1,1920]{3,2,1,0:T(1,128)} async-done(((f32[128,1,1,1920]{3,2,1,0:T(1,128)}), f32[128,1,1,1920]{3,2,1,0:T(1,128)}, u32[]{:S(2)}, u32[]{:S(2)}) %all-to-all-start) | async-done | bytes 983072 | tf_op jit(solution)/shard_map/all_to_all | solution.py:42
  50.0 9.2 %all_to_all.72 = f32[1,128,1,1920]{3,2,0,1:T(1,128)} all-to-all(f32[1,128,1,1920]{3,2,0,1:T(1,128)} %bitcast.3), channel_id=1, replica_groups=mesh['dp'=128,'tensor'=2] {'tensor'}, dimensions={1} | all-to-all | bytes 1966080 | tf_op jit(solution)/shard_map/all_to_all | solution.py:41
  59.2 8.5 %all-to-all-start.2 = ((f32[128,1,1,1920]{3,2,1,0:T(1,128)}), f32[128,1,1,1920]{3,2,1,0:T(1,128)}, u32[]{:S(2)}, u32[]{:S(2)}) async-start(f32[128,1,1,1920]{3,2,1,0:T(1,128)} %copy.43), calls=%async_computation.2 | async-start | bytes 1966080 | tf_op jit(solution)/shard_map/all_to_all | solution.py:54
  67.7 3.6 %reshape.58 = f32[8,6,128,40]{3,2,0,1:T(8,128)S(1)} reshape(f32[8,6,5120]{2,0,1:T(8,128)} %param.6) | data formatting | bytes 1966080 | tf_op jit(solution)/shard_map/reshape | solution.py:18
  71.4 1.9 copy.49
  73.3 3.2 %copy.50 = f32[128,1,1,1920]{3,2,1,0:T(1,128)} copy(f32[128,1,1,1920]{0,3,2,1:T(8,128)} %bitcast.59) | data formatting | bytes 1966080 | tf_op jit(solution)/shard_map/reshape | solution.py:20
  76.5 18.2 %all-to-all-done.2 = f32[128,1,1,1920]{3,2,1,0:T(1,128)} async-done(((f32[128,1,1,1920]{3,2,1,0:T(1,128)}), f32[128,1,1,1920]{3,2,1,0:T(1,128)}, u32[]{:S(2)}, u32[]{:S(2)}) %all-to-all-start.2) | async-done | bytes 983072 | tf_op jit(solution)/shard_map/all_to_all | solution.py:54
  94.7 7.3 %all_to_all.73 = f32[1,128,1,1920]{3,2,0,1:T(1,128)S(1)} all-to-all(f32[1,128,1,1920]{3,2,0,1:T(1,128)} %bitcast.11), channel_id=1, replica_groups=mesh['dp'=128,'tensor'=2] {'tensor'}, dimensions={1} | all-to-all | bytes 1966080 | tf_op jit(solution)/shard_map/all_to_all | solution.py:53
  101.9 0.0 copy-start.3
  101.9 7.9 %all-to-all-start.4 = ((f32[128,1,1,1920]{3,2,1,0:T(1,128)}), f32[128,1,1,1920]{3,2,1,0:T(1,128)S(1)}, u32[]{:S(2)}, u32[]{:S(2)}) async-start(f32[128,1,1,1920]{3,2,1,0:T(1,128)} %copy.50), calls=%async_computation.4 | async-start | bytes 1966080 | tf_op jit(solution)/shard_map/all_to_all | solution.py:68
  109.8 2.1 multiply_reduce_fusion
  111.9 77.6 %psum.7 = f32[]{:T(128)} all-reduce(f32[]{:T(128)} %multiply_reduce_fusion), channel_id=1, replica_groups=mesh['dp'=128,'tensor'=2] {'dp','tensor'}, use_global_device_ids=true, to_apply=%region_1.0 | all-reduce | flops 1 | bytes 8 | tf_op jit(solution)/shard_map/psum | solution.py:35
  189.5 3.2 %copy.48 = f32[8,40,768]{1,0,2:T(8,128)} copy(f32[8,40,768]{2,1,0:T(8,128)} %param.7) | data formatting | bytes 1966080 | tf_op args[3]
  193.4 0.0 copy-done.3
  193.4 0.1 copy_multiply_fusion.2
  193.5 1.7 copy.40
  195.2 0.1 copy_multiply_fusion.1
  195.4 1.7 copy.46
  197.1 0.0 all-to-all-done.4
  197.1 5.1 %all_to_all.74 = f32[1,128,1,1920]{3,2,0,1:T(1,128)S(1)} all-to-all(f32[1,128,1,1920]{3,2,0,1:T(1,128)S(1)} %bitcast.53), channel_id=1, replica_groups=mesh['dp'=128,'tensor'=2] {'tensor'}, dimensions={1} | all-to-all | bytes 1966080 | tf_op jit(solution)/shard_map/all_to_all | solution.py:67
  202.1 0.1 copy_multiply_fusion
  202.3 0.8 copy.53
  203.0 4.1 %mul.98 = f32[128,8,6,40]{3,2,1,0:T(8,128)} reshape(f32[1,64,2,1,1920]{4,2,1,3,0:T(2,128)S(1)} %copy.53) | data formatting | bytes 1966080 | tf_op jit(solution)/shard_map/mul | solution.py:82
  207.2 2.9 %copy.54 = f32[8,40,128,6]{1,0,3,2:T(8,128)S(1)} copy(f32[8,40,128,6]{1,3,0,2:T(8,128)} %bitcast.47) | data formatting | bytes 1966080 | tf_op jit(solution)/shard_map/mul | solution.py:82
  210.1 4.7 %mul.87 = f32[128,8,6,40]{3,2,1,0:T(8,128)} reshape(f32[1,64,2,1,1920]{4,2,1,3,0:T(2,128)} %copy.46) | data formatting | bytes 1966080 | tf_op jit(solution)/shard_map/mul | solution.py:81
  214.8 4.7 %copy.47 = f32[8,40,128,6]{1,0,3,2:T(8,128)} copy(f32[8,40,128,6]{1,3,0,2:T(8,128)} %bitcast.48) | data formatting | bytes 1966080 | tf_op jit(solution)/shard_map/mul | solution.py:81
  219.5 4.7 %mul.81 = f32[128,8,6,40]{3,2,1,0:T(8,128)} reshape(f32[1,64,2,1,1920]{4,2,1,3,0:T(2,128)} %copy.40) | data formatting | bytes 1966080 | tf_op jit(solution)/shard_map/mul | solution.py:84
  224.2 0.0 copy-start
  224.2 0.0 copy-start.1
  224.2 3.1 %copy.41 = f32[8,40,128,6]{1,0,3,2:T(8,128)S(1)} copy(f32[8,40,128,6]{1,3,0,2:T(8,128)} %bitcast.49) | data formatting | bytes 1966080 | tf_op jit(solution)/shard_map/mul | solution.py:84
  227.3 0.0 copy-done
  227.3 1.0 copy-done.1
  228.3 4.8 %bitcast_subtract_fusion = (f32[8,40,768]{1,0,2:T(8,128)}, f32[8,40,768]{1,0,2:T(8,128)}, f32[8,40,768]{1,0,2:T(8,128)}) fusion(f32[8,40,128,6]{1,0,3,2:T(8,128)S(1)} %copy.41, f32[8,40,768]{1,0,2:T(8,128)S(1)} %copy-done.1, f32[]{:T(128)S(6)} %min_shard_map.3, f32[8,40,128,6]{1,0,3,2:T(8,128)S(1)} %copy-done, f32[8,40,128,6]{1,0,3,2:T(8,128)S(1)} %copy.54), kind=kLoop, calls=%fused_computation.3 | loop fusion | flops 2949120 | bytes 6881284 | tf_op jit(solution)/shard_map/sub | solution.py:84
  233.1 0.0 copy-start.2
  233.1 3.3 %copy.55 = f32[8,40,768]{2,1,0:T(8,128)} copy(f32[8,40,768]{1,0,2:T(8,128)} %get-tuple-element.12) | data formatting | bytes 1966080
  236.4 3.1 %copy.56 = f32[8,40,768]{2,1,0:T(8,128)} copy(f32[8,40,768]{1,0,2:T(8,128)} %get-tuple-element.13) | data formatting | bytes 1966080
  239.5 0.0 copy-done.2
  239.5 1.9 copy.57
Async XLA Ops:
  9.4 40.6 %all-to-all-start = ((f32[128,1,1,1920]{3,2,1,0:T(1,128)}), f32[128,1,1,1920]{3,2,1,0:T(1,128)}, u32[]{:S(2)}, u32[]{:S(2)}) async-start(f32[128,1,1,1920]{3,2,1,0:T(1,128)} %copy.37), calls=%async_computation | async-start | bytes 1966080 | tf_op jit(solution)/shard_map/all_to_all | solution.py:42
  59.2 35.5 %all-to-all-start.2 = ((f32[128,1,1,1920]{3,2,1,0:T(1,128)}), f32[128,1,1,1920]{3,2,1,0:T(1,128)}, u32[]{:S(2)}, u32[]{:S(2)}) async-start(f32[128,1,1,1920]{3,2,1,0:T(1,128)} %copy.43), calls=%async_computation.2 | async-start | bytes 1966080 | tf_op jit(solution)/shard_map/all_to_all | solution.py:54
  101.9 91.5 %copy-start.3 = (f32[1,128,1,1920]{3,2,0,1:T(1,128)S(1)}, f32[1,128,1,1920]{3,2,0,1:T(1,128)}, u32[]{:S(2)}) copy-start(f32[1,128,1,1920]{3,2,0,1:T(1,128)} %all_to_all.72) | copy-start | bytes 2949124
  101.9 95.1 %all-to-all-start.4 = ((f32[128,1,1,1920]{3,2,1,0:T(1,128)}), f32[128,1,1,1920]{3,2,1,0:T(1,128)S(1)}, u32[]{:S(2)}, u32[]{:S(2)}) async-start(f32[128,1,1,1920]{3,2,1,0:T(1,128)} %copy.50), calls=%async_computation.4 | async-start | bytes 1966080 | tf_op jit(solution)/shard_map/all_to_all | solution.py:68
  224.2 3.2 %copy-start = (f32[8,40,128,6]{1,0,3,2:T(8,128)S(1)}, f32[8,40,128,6]{1,0,3,2:T(8,128)}, u32[]{:S(2)}) copy-start(f32[8,40,128,6]{1,0,3,2:T(8,128)} %copy.47) | copy-start | bytes 2949124
  224.2 4.1 %copy-start.1 = (f32[8,40,768]{1,0,2:T(8,128)S(1)}, f32[8,40,768]{1,0,2:T(8,128)}, u32[]{:S(2)}) copy-start(f32[8,40,768]{1,0,2:T(8,128)} %copy.48) | copy-start | bytes 2949124
  233.1 6.4 %copy-start.2 = (f32[8,40,768]{1,0,2:T(8,128)S(1)}, f32[8,40,768]{1,0,2:T(8,128)}, u32[]{:S(2)}) copy-start(f32[8,40,768]{1,0,2:T(8,128)} %get-tuple-element.14) | copy-start | bytes 2949124
where the time goes:
time: 245 us; the launch traced here: 241 us
  blocking collectives  99.1 us (40%)
  local copies, waits for them, and re-layouts  67.2 us (27%)
  waiting for transfers between devices  35.5 us (14%)
  starting transfers between devices  30.9 us (13%)
  other arithmetic  7.23 us (3%)
    psum x1, blocking collectives, local(): total = lax.psum(local_sum, ('dp', 'tensor'))  77.6 us
    all_to_all x1, waiting for transfers between devices, local(): lax.all_to_all(prepare(moment_one, owners), 'dp', split_axis=0, concat_ax...  18.2 us
    all_to_all x1, waiting for transfers between devices, local(): lax.all_to_all(prepare(master, owners), 'dp', split_axis=0, concat_axis=1...  17.3 us
    all_to_all x1, starting transfers between devices, local(): lax.all_to_all(prepare(master, owners), 'dp', split_axis=0, concat_axis=1...  14.5 us
    unnamed x12, local copies, waits for them, and re-layouts  12.5 us
    mul x3, local copies, waits for them, and re-layouts, local(): new_first = 0.9 * first + 0.1 * clipped  11.1 us
    reshape x3, local copies, waits for them, and re-layouts, prepare(): split = stored.reshape(mats, rows, owners, block)  10.9 us
    reshape x3, local copies, waits for them, and re-layouts, prepare(): return grouped.reshape(owners, 1, 1, mats * rows * block)  9.63 us
  transfers between devices with their start and end apart: 3, of which 2 were waited for; matrix products, arithmetic and copies ran while one was open for 11% of the time, Pallas kernels for 0%

commit v1 on v0

v1 whole, which is shorter than its diff:
```python
import jax
import jax.numpy as jnp
from jax import lax
from jax.experimental import pallas as pl
from jax.experimental.pallas import tpu as pltpu
from jax.sharding import PartitionSpec as P

D = 5120
MOE_FF = 1536
MATS = 8
ROWS = 6
BLOCK = 40
MESH = pl.DeviceIdType.MESH

bias_first = 0.9999734386011124
bias_second = 0.994079470779666
COUNT = float(MATS * D * MOE_FF)


def pack_group(xin, src, zt, part):
    lane = lax.broadcasted_iota(jnp.int32, (8, 128), 1)
    base = pl.multiple_of(zt * 640, 128)
    for h in range(ROWS):
        tiles = []
        for a in range(3):
            row = []
            for t in range(5):
                v = xin[a, h, :, pl.ds(base + 128 * t, 128)]
                row.append(v if a == 0 else pltpu.roll(v, 40 * a, 1))
            tiles.append(row)
        for p in range(16):
            start = (40 * p) % 128
            t0 = (40 * p) // 128
            u = (lane + (128 - start)) & 127
            pieces = []
            for a in range(3):
                piece = tiles[a][t0]
                if start + 40 > 128:
                    piece = jnp.where(u < 40 * a + 128 - start, piece, tiles[a][t0 + 1])
                pieces.append(piece)
            out = jnp.where(u < 40, pieces[0], jnp.where(u < 80, pieces[1], pieces[2]))
            if h == 0:
                out = jnp.where(u < 120, out, part)
            src[zt * 16 + p, 8 * h : 8 * h + 8, :] = out


def kernel(
    x0, x1, x2, g_hbm, o0, o1, o2,
    xin, gv, src, arr, wide, outv, sumv, sib,
    in_sem, g_sem, send_sem, recv_sem, sib_send, sib_recv, out_sem,
):
    s = lax.axis_index("dp")
    c = lax.axis_index("tensor")
    z = s // 16
    plane = s % 16
    half = z // 4
    dl = 2 * (s % 64) + c
    group = (z % 4) // 2
    mine = half == c

    gcopy = pltpu.make_async_copy(g_hbm, gv, g_sem)
    gcopy.start()

    def in_copies(zt):
        cols = pl.ds(pl.multiple_of(zt * 640, 128), 640)
        return [
            pltpu.make_async_copy(x.at[:, :, cols], xin.at[a, :, :, cols], in_sem.at[zt])
            for a, x in enumerate((x0, x1, x2))
        ]

    def order(i):
        return 2 * (1 - i % 2) + (1 - i // 2)

    def start_in(j, carry):
        for copy in in_copies(z ^ (2 * order(j // 2) + j % 2)):
            copy.start()
        return carry

    lax.fori_loop(0, 8, start_in, 0)

    barrier = pltpu.get_barrier_semaphore()

    def greet(i, carry):
        peer, core = c * 64 + i // 2, i % 2

        @pl.when(jnp.logical_or(peer != s, core != c))
        def _():
            pl.semaphore_signal(barrier, inc=1, device_id=(peer, core), device_id_type=MESH)

        return carry

    lax.fori_loop(0, 128, greet, 0)

    @pl.when(jnp.logical_not(mine))
    def _():
        pl.semaphore_signal(barrier, inc=1, device_id=(s, 1 - c), device_id_type=MESH)

    gcopy.wait()

    def squares(m, acc):
        for i in range(5):
            for j in range(6):
                v = gv[m, 8 * i : 8 * i + 8, 128 * j : 128 * j + 128]
                acc = acc + v * v
        return acc

    acc = lax.fori_loop(0, MATS, squares, jnp.zeros((8, 128), jnp.float32))
    part = jnp.broadcast_to(jnp.sum(acc, axis=(0, 1), keepdims=True), (8, 128))

    def message(t):
        return pltpu.make_async_remote_copy(
            src_ref=src.at[t],
            dst_ref=arr.at[pl.ds(pl.multiple_of(48 * dl, 8), 48)],
            send_sem=send_sem,
            recv_sem=recv_sem.at[group],
            device_id=(t, half),
            device_id_type=MESH,
        )

    def phase(i, carry):
        a = order(i)

        def pack(e, inner):
            zt = z ^ (2 * a + e)
            for copy in in_copies(zt):
                copy.wait()
            pack_group(xin, src, zt, part)
            return inner

        lax.fori_loop(0, 2, pack, 0)

        @pl.when(i == 0)
        def _():
            pl.semaphore_wait(barrier, 128)

        def send(r, inner):
            t = (z ^ (2 * a + r % 2)) * 16 + (plane ^ (r // 2))
            own = jnp.logical_and(t == s, mine)

            @pl.when(jnp.logical_not(own))
            def _():
                message(t).start()

            @pl.when(own)
            def _():
                pltpu.make_async_copy(
                    src.at[t], arr.at[pl.ds(pl.multiple_of(48 * dl, 8), 48)], recv_sem.at[group]
                ).start()

            return inner

        lax.fori_loop(0, 32, send, 0)
        return carry

    lax.fori_loop(0, 4, phase, 0)

    def gather(i, carry):
        first = (z // 2) ^ jnp.where(mine, 1, 3)
        grp = jnp.where(i == 0, first, first ^ 1) % 2
        rows = pl.ds(pl.multiple_of(grp * 3072, 8), 3072)
        pltpu.make_async_copy(arr.at[rows], arr.at[rows], recv_sem.at[grp]).wait()

        def flip(m, inner):
            for t in range(3):
                tile = grp * 3 + t
                x = arr[pl.ds(tile * 1024 + m, 128, 8), :]
                wide[tile, m] = x.T
            return inner

        lax.fori_loop(0, MATS, flip, 0)
        return carry

    lax.fori_loop(0, 2, gather, 0)

    def partial(d, acc):
        return acc + arr[pl.ds(pl.multiple_of(d * 48, 8), 8), :]

    halves = lax.fori_loop(0, 128, partial, jnp.zeros((8, 128), jnp.float32))
    lane = lax.broadcasted_iota(jnp.int32, (8, 128), 1)
    sub = lax.broadcasted_iota(jnp.int32, (8, 128), 0)
    begin = (40 * plane) % 128
    spot = jnp.logical_and((lane + (128 - begin)) % 128 == 120, sub == 0)
    half_sum = jnp.sum(jnp.where(spot, halves, 0.0), axis=(0, 1), keepdims=True)
    sumv[...] = jnp.broadcast_to(half_sum, (8, 128))
    swap = pltpu.make_async_remote_copy(
        src_ref=sumv,
        dst_ref=sib,
        send_sem=sib_send,
        recv_sem=sib_recv,
        device_id=(s, 1 - c),
        device_id_type=MESH,
    )
    swap.start()
    swap.wait()
    total = (sumv[...] + sib[...])[0:1, 0:1]
    scale = jnp.minimum(1.0, 0.5 * jnp.sqrt(jnp.float32(COUNT)) / (jnp.sqrt(total) + 1e-06))
    scale = jnp.broadcast_to(scale, (8, 128))

    def out_copies(m):
        return [
            pltpu.make_async_copy(outv.at[a, m], o.at[m], out_sem) for a, o in enumerate((o0, o1, o2))
        ]

    def update(m, carry):
        for w in range(5):
            spots = [pl.multiple_of(8 * ((5 * plane + 5 * a + w) % 16), 8) for a in range(3)]
            for t in range(6):
                rows = slice(8 * w, 8 * w + 8)
                cols = slice(128 * t, 128 * t + 128)
                weights = wide[t, m, pl.ds(spots[0], 8), :]
                first = wide[t, m, pl.ds(spots[1], 8), :]
                second = wide[t, m, pl.ds(spots[2], 8), :]
                clipped = scale * gv[m, rows, cols]
                new_first = 0.9 * first + 0.1 * clipped
                new_second = 0.95 * second + 0.05 * clipped * clipped
                step = new_first / bias_first / (jnp.sqrt(new_second / bias_second) + 1e-08)
                outv[0, m, rows, cols] = weights * (1.0 - 0.05 * 0.1) - 0.05 * step
                outv[1, m, rows, cols] = new_first
                outv[2, m, rows, cols] = new_second
        for copy in out_copies(m):
            copy.start()
        return carry

    lax.fori_loop(0, MATS, update, 0)
    for a, o in enumerate((o0, o1, o2)):
        pltpu.make_async_copy(outv.at[a], o, out_sem).wait()
    pltpu.make_async_copy(src.at[pl.ds(0, 127)], src.at[pl.ds(0, 127)], send_sem).wait()

    @pl.when(jnp.logical_not(mine))
    def _():
        pltpu.make_async_copy(src.at[127], src.at[127], send_sem).wait()


def local(master, moment_one, moment_two, grad):
    shape = jax.ShapeDtypeStruct(grad.shape, jnp.float32)
    hbm = pl.BlockSpec(memory_space=pl.ANY)
    stored = [jnp.transpose(x, (1, 0, 2)) for x in (master, moment_one, moment_two)]
    return pl.pallas_call(
        kernel,
        name="regroup_adamw",
        out_shape=(shape, shape, shape),
        in_specs=[hbm] * 4,
        out_specs=(hbm, hbm, hbm),
        scratch_shapes=[
            pltpu.VMEM((3, ROWS, MATS, D), jnp.float32),
            pltpu.VMEM((MATS, BLOCK, 768), jnp.float32),
            pltpu.VMEM((128, 48, 128), jnp.float32),
            pltpu.VMEM((128 * 48, 128), jnp.float32),
            pltpu.VMEM((6, MATS, 128, 128), jnp.float32),
            pltpu.VMEM((3, MATS, BLOCK, 768), jnp.float32),
            pltpu.VMEM((8, 128), jnp.float32),
            pltpu.VMEM((8, 128), jnp.float32),
            pltpu.SemaphoreType.DMA((8,)),
            pltpu.SemaphoreType.DMA,
            pltpu.SemaphoreType.DMA,
            pltpu.SemaphoreType.DMA((2,)),
            pltpu.SemaphoreType.DMA,
            pltpu.SemaphoreType.DMA,
            pltpu.SemaphoreType.DMA,
        ],
        compiler_params=pltpu.CompilerParams(
            collective_id=0, has_side_effects=True, vmem_limit_bytes=40 * 2**20
        ),
        cost_estimate=pl.CostEstimate(
            flops=8_000_000, bytes_accessed=7_000_000, transcendentals=500_000
        ),
    )(*stored, grad)


def solution(mesh):
    placed = (
        P(None, ("dp", "tensor"), None),
        P(None, ("dp", "tensor"), None),
        P(None, ("dp", "tensor"), None),
        P(None, "dp", "tensor"),
    )
    return jax.shard_map(
        local,
        mesh=mesh,
        in_specs=placed,
        out_specs=(P(None, "dp", "tensor"), P(None, "dp", "tensor"), P(None, "dp", "tensor")),
        check_vma=False,
    )
```

time: 245 us -> 105 us (0.43); the launches traced: 241 us -> 105 us
  blocking collectives: 99.1 us -> 0 us
  Pallas kernels: 0 us -> 96.3 us
  local copies, waits for them, and re-layouts: 67.2 us -> 7.63 us
  waiting for transfers between devices: 35.5 us -> 0 us
  starting transfers between devices: 30.9 us -> 0 us
  other arithmetic: 7.23 us -> 0 us
    pallas_call x0 -> x1, Pallas kernels: none -> 96.3 us  [local(): pl.pallas_call(kernel, name='regroup_adamw', out_shape=(shape, shape, sha...]
    psum x1 -> x0, blocking collectives: 77.6 us -> none  [local(): total = lax.psum(local_sum, ('dp', 'tensor'))]
    all_to_all x3 -> x0, waiting for transfers between devices: 35.5 us -> none  [the longest x1 18.2 us: local(): lax.all_to_all(prepare(moment_one, owners), 'dp', split_axis=0, concat_ax...]
    all_to_all x3 -> x0, starting transfers between devices: 30.9 us -> none  [the longest x1 14.5 us: local(): lax.all_to_all(prepare(master, owners), 'dp', split_axis=0, concat_axis=1...]
    mul x9 -> x0, local copies, waits for them, and re-layouts: 28.5 us -> none  [the longest x3 11.1 us: local(): new_first = 0.9 * first + 0.1 * clipped]
    all_to_all x3 -> x0, blocking collectives: 21.6 us -> none  [the longest x1 9.23 us: local(): lax.all_to_all(lax.all_to_all(prepare(master, owners), 'dp', split_axis=0...]
    reshape x6 -> x0, local copies, waits for them, and re-layouts: 20.6 us -> none  [the longest x3 10.9 us: prepare(): split = stored.reshape(mats, rows, owners, block)]
    transpose x3 -> x0, local copies, waits for them, and re-layouts: 5.72 us -> none  [prepare(): grouped = jnp.transpose(split, (2, 0, 1, 3))]
  transfers between devices with their start and end apart: 3 -> 0, of which waited for: 2 -> 0; matrix products, arithmetic and copies ran while one was open for 11% -> 0% of each run, Pallas kernels for 0% -> 0%
where the time goes in v1:
time: 105 us
  Pallas kernels  96.3 us (92%)
  local copies, waits for them, and re-layouts  7.63 us (7%)
    pallas_call x1, Pallas kernels, local(): pl.pallas_call(kernel, name='regroup_adamw', out_shape=(shape, shape, sha...  96.3 us
    unnamed x11, local copies, waits for them, and re-layouts  7.63 us

profile of v1, /device:TPU:65, one launch (start us, length us, event | category | flops | bytes accessed | tf_op | source)
XLA Modules:
  0.0 104.5 jit_solution(8015127704193416482)
XLA Ops:
  0.6 0.0 copy-start
  0.6 1.2 %copy-done = f32[8,6,5120]{2,0,1:T(8,128)S(1)} copy-done((f32[8,6,5120]{2,0,1:T(8,128)S(1)}, f32[8,6,5120]{2,0,1:T(8,128)}, u32[]{:S(2)}) %copy-start) | copy-done | bytes 983064
  1.8 0.0 copy-start.1
  1.8 1.2 %copy-done.1 = f32[8,6,5120]{2,0,1:T(8,128)S(1)} copy-done((f32[8,6,5120]{2,0,1:T(8,128)S(1)}, f32[8,6,5120]{2,0,1:T(8,128)}, u32[]{:S(2)}) %copy-start.1) | copy-done | bytes 983064
  3.0 0.0 copy-start.2
  3.0 1.2 %copy-done.2 = f32[8,6,5120]{2,0,1:T(8,128)S(1)} copy-done((f32[8,6,5120]{2,0,1:T(8,128)S(1)}, f32[8,6,5120]{2,0,1:T(8,128)}, u32[]{:S(2)}) %copy-start.2) | copy-done | bytes 983064
  4.2 0.0 copy-start.3
  4.2 1.2 %copy-done.3 = f32[8,40,768]{2,1,0:T(8,128)S(1)} copy-done((f32[8,40,768]{2,1,0:T(8,128)S(1)}, f32[8,40,768]{2,1,0:T(8,128)}, u32[]{:S(2)}) %copy-start.3) | copy-done | bytes 983064
  5.4 96.3 %regroup_adamw.1 = (f32[8,40,768]{2,1,0:T(8,128)S(1)}, f32[8,40,768]{2,1,0:T(8,128)S(1)}, f32[8,40,768]{2,1,0:T(8,128)S(1)}) custom-call(f32[6,8,5120]{2,1,0:T(8,128)S(1)} %bitcast.3, f32[6,8,5120]{2,1,0:T(8,128)S(1)} %bitcast.4, f32[6,8,5120]{2,1,0:T(8,128)S(1)} %bitcast.5, f32[8,40,768]{2,1,0:T(8,128)S(1)} %copy-done.3), custom_call_target="tpu_custom_call" | custom-call | flops 8000000 | bytes 7000000 | tf_op jit(solution)/shard_map/regroup_adamw/pallas_call | solution.py:238
  101.7 0.9 copy.10
  102.6 0.9 copy.11
  103.6 0.9 copy.12
Async XLA Ops:
  0.6 1.2 %copy-start = (f32[8,6,5120]{2,0,1:T(8,128)S(1)}, f32[8,6,5120]{2,0,1:T(8,128)}, u32[]{:S(2)}) copy-start(f32[8,6,5120]{2,0,1:T(8,128)} %param.4) | copy-start | bytes 2949124
  1.8 1.2 %copy-start.1 = (f32[8,6,5120]{2,0,1:T(8,128)S(1)}, f32[8,6,5120]{2,0,1:T(8,128)}, u32[]{:S(2)}) copy-start(f32[8,6,5120]{2,0,1:T(8,128)} %param.5) | copy-start | bytes 2949124
  3.0 1.2 %copy-start.2 = (f32[8,6,5120]{2,0,1:T(8,128)S(1)}, f32[8,6,5120]{2,0,1:T(8,128)}, u32[]{:S(2)}) copy-start(f32[8,6,5120]{2,0,1:T(8,128)} %param.6) | copy-start | bytes 2949124
  4.2 1.2 %copy-start.3 = (f32[8,40,768]{2,1,0:T(8,128)S(1)}, f32[8,40,768]{2,1,0:T(8,128)}, u32[]{:S(2)}) copy-start(f32[8,40,768]{2,1,0:T(8,128)} %g_hbm.1) | copy-start | bytes 2949124

commit v2 on v1

v2 whole, which is shorter than its diff:
```python
import jax
import jax.numpy as jnp
from jax import lax
from jax.experimental import pallas as pl
from jax.experimental.pallas import tpu as pltpu
from jax.sharding import PartitionSpec as P

D = 5120
MOE_FF = 1536
MATS = 8
ROWS = 6
BLOCK = 40
MESH = pl.DeviceIdType.MESH

bias_first = 0.9999734386011124
bias_second = 0.994079470779666
COUNT = float(MATS * D * MOE_FF)


def pack_group(xin, src, zt):
    lane = lax.broadcasted_iota(jnp.int32, (8, 128), 1)
    base = pl.multiple_of(zt * 640, 128)
    for h in range(ROWS):
        tiles = []
        for a in range(3):
            row = []
            for t in range(5):
                v = xin[a, h, :, pl.ds(base + 128 * t, 128)]
                row.append(v if a == 0 else pltpu.roll(v, 40 * a, 1))
            tiles.append(row)
        for p in range(16):
            start = (40 * p) % 128
            t0 = (40 * p) // 128
            u = (lane + (128 - start)) & 127
            pieces = []
            for a in range(3):
                piece = tiles[a][t0]
                if start + 40 > 128:
                    piece = jnp.where(u < 40 * a + 128 - start, piece, tiles[a][t0 + 1])
                pieces.append(piece)
            out = jnp.where(u < 40, pieces[0], jnp.where(u < 80, pieces[1], pieces[2]))
            src[zt * 16 + p, 8 * h : 8 * h + 8, :] = out


def regroup(
    x0, x1, x2, g_hbm, wide, gv, total,
    xin, src, arr, mine_sum, plane_sums, col_sums, sib_sum,
    in_sem, g_sem, send_sem, recv_sem, small_send, plane_recv, col_recv, sib_recv, col_sem,
):
    s = lax.axis_index("dp")
    c = lax.axis_index("tensor")
    z = s // 16
    plane = s % 16
    half = z // 4
    dl = 2 * (s % 64) + c
    mine = half == c

    barrier = pltpu.get_barrier_semaphore()
    for i in range(1, 16):
        for core in range(2):
            pl.semaphore_signal(barrier, inc=1, device_id=(s ^ i, core), device_id_type=MESH)
    for i in range(1, 8):
        pl.semaphore_signal(barrier, inc=1, device_id=(s ^ (16 * i), c), device_id_type=MESH)
    pl.semaphore_signal(barrier, inc=1, device_id=(s, 1 - c), device_id_type=MESH)

    def in_copies(zt):
        cols = pl.ds(pl.multiple_of(zt * 640, 128), 640)
        return [
            pltpu.make_async_copy(x.at[:, :, cols], xin.at[a, :, :, cols], in_sem.at[zt])
            for a, x in enumerate((x0, x1, x2))
        ]

    for zt in range(8):
        for copy in in_copies(zt):
            copy.start()
    gcopy = pltpu.make_async_copy(g_hbm, gv, g_sem)
    gcopy.start()

    def pack(zt, carry):
        for copy in in_copies(zt):
            copy.wait()
        pack_group(xin, src, zt)
        return carry

    lax.fori_loop(0, 4, pack, 0)
    pl.semaphore_wait(barrier, 38)
    for i in range(1, 8):
        pl.semaphore_signal(col_sem, inc=1, device_id=(s ^ (16 * i), c), device_id_type=MESH)
    lax.fori_loop(4, 8, pack, 0)
    pl.semaphore_wait(col_sem, 7)

    slot = arr.at[pl.ds(pl.multiple_of(48 * dl, 8), 48)]

    def send(j, carry):
        for e in range(8):
            t = s ^ (16 * (7 - e)) ^ (j ^ (2 * e))
            message = pltpu.make_async_remote_copy(
                src_ref=src.at[t],
                dst_ref=slot,
                send_sem=send_sem,
                recv_sem=recv_sem,
                device_id=(t, half),
                device_id_type=MESH,
            )
            if e < 7:
                message.start()
            else:
                own = jnp.logical_and(j == 14, mine)
                pl.when(jnp.logical_not(own))(message.start)
                pl.when(own)(pltpu.make_async_copy(src.at[t], slot, recv_sem).start)
        return carry

    def small(dst, recv, peer, core):
        return pltpu.make_async_remote_copy(
            src_ref=mine_sum,
            dst_ref=dst,
            send_sem=small_send,
            recv_sem=recv,
            device_id=(peer, core),
            device_id_type=MESH,
        )

    lax.fori_loop(0, 2, send, 0)

    gcopy.wait()

    def squares(m, acc):
        for i in range(5):
            for j in range(6):
                v = gv[m, 8 * i : 8 * i + 8, 128 * j : 128 * j + 128]
                acc = acc + v * v
        return acc

    acc = lax.fori_loop(0, MATS, squares, jnp.zeros((8, 128), jnp.float32))
    part = jnp.broadcast_to(jnp.sum(acc, axis=(0, 1), keepdims=True), (1, 128))
    mine_sum[0] = part
    plane_sums[plane] = part
    plane_out = [small(plane_sums.at[pl.ds(plane, 1)], plane_recv, s ^ i, c) for i in range(1, 16)]
    for copy in plane_out:
        copy.start()
    lax.fori_loop(2, 8, send, 0)
    for copy in plane_out:
        copy.wait_send()
    first15 = plane_sums.at[pl.ds(0, 15)]
    pltpu.make_async_copy(first15, first15, plane_recv).wait()
    part = jnp.sum(plane_sums[...], axis=0)
    mine_sum[0] = part
    col_sums[z] = part
    col_out = [small(col_sums.at[pl.ds(z, 1)], col_recv, s ^ (16 * i), c) for i in range(1, 8)]
    for copy in col_out:
        copy.start()
    lax.fori_loop(8, 16, send, 0)
    for copy in col_out:
        copy.wait_send()
    first7 = col_sums.at[pl.ds(0, 7)]
    pltpu.make_async_copy(first7, first7, col_recv).wait()
    part = jnp.sum(col_sums[...], axis=0)
    mine_sum[0] = part
    swap = small(sib_sum, sib_recv, s, 1 - c)
    swap.start()
    swap.wait()
    total[...] = part + sib_sum[0]

    pltpu.make_async_copy(arr, arr, recv_sem).wait()

    def flip(m, carry):
        for t in range(6):
            wide[t, m] = arr[pl.ds(t * 1024 + m, 128, 8), :].T
        return carry

    lax.fori_loop(0, MATS, flip, 0)

    sent = src.at[pl.ds(0, 127)]
    pltpu.make_async_copy(sent, sent, send_sem).wait()

    @pl.when(jnp.logical_not(mine))
    def _():
        pltpu.make_async_copy(src.at[127], src.at[127], send_sem).wait()


def adamw(wide, gv, total, o0, o1, o2, outv, out_sem):
    plane = lax.axis_index("dp") % 16
    limit = 0.5 * jnp.sqrt(jnp.float32(COUNT))
    scale = jnp.minimum(1.0, limit / (jnp.sqrt(total[...]) + 1e-06))
    scale = jnp.broadcast_to(scale, (8, 128))

    def update(m, carry):
        for w in range(5):
            spots = [pl.multiple_of(8 * ((5 * plane + 5 * a + w) % 16), 8) for a in range(3)]
            for t in range(6):
                rows = slice(8 * w, 8 * w + 8)
                cols = slice(128 * t, 128 * t + 128)
                weights = wide[t, m, pl.ds(spots[0], 8), :]
                first = wide[t, m, pl.ds(spots[1], 8), :]
                second = wide[t, m, pl.ds(spots[2], 8), :]
                clipped = scale * gv[m, rows, cols]
                new_first = 0.9 * first + 0.1 * clipped
                new_second = 0.95 * second + 0.05 * clipped * clipped
                step = new_first / bias_first / (jnp.sqrt(new_second / bias_second) + 1e-08)
                outv[0, m, rows, cols] = weights * (1.0 - 0.05 * 0.1) - 0.05 * step
                outv[1, m, rows, cols] = new_first
                outv[2, m, rows, cols] = new_second
        for a, o in enumerate((o0, o1, o2)):
            pltpu.make_async_copy(outv.at[a, m], o.at[m], out_sem).start()
        return carry

    lax.fori_loop(0, MATS, update, 0)
    for a, o in enumerate((o0, o1, o2)):
        pltpu.make_async_copy(outv.at[a], o, out_sem).wait()


def local(master, moment_one, moment_two, grad):
    shape = jax.ShapeDtypeStruct(grad.shape, jnp.float32)
    hbm = pl.BlockSpec(memory_space=pltpu.HBM)
    vmem = pl.BlockSpec(memory_space=pltpu.VMEM)
    stored = [
        pltpu.with_memory_space_constraint(jnp.transpose(x, (1, 0, 2)), pltpu.HBM)
        for x in (master, moment_one, moment_two)
    ]
    grad = pltpu.with_memory_space_constraint(grad, pltpu.HBM)
    wide, gv, total = pl.pallas_call(
        regroup,
        name="regroup",
        out_shape=(
            pltpu.VMEM((6, MATS, 128, 128), jnp.float32),
            pltpu.VMEM(grad.shape, jnp.float32),
            pltpu.VMEM((1, 128), jnp.float32),
        ),
        in_specs=[hbm] * 4,
        out_specs=(vmem, vmem, vmem),
        scratch_shapes=[
            pltpu.VMEM((3, ROWS, MATS, D), jnp.float32),
            pltpu.VMEM((128, 48, 128), jnp.float32),
            pltpu.VMEM((128 * 48, 128), jnp.float32),
            pltpu.VMEM((1, 1, 128), jnp.float32),
            pltpu.VMEM((16, 1, 128), jnp.float32),
            pltpu.VMEM((8, 1, 128), jnp.float32),
            pltpu.VMEM((1, 1, 128), jnp.float32),
            pltpu.SemaphoreType.DMA((8,)),
            pltpu.SemaphoreType.DMA,
            pltpu.SemaphoreType.DMA,
            pltpu.SemaphoreType.DMA,
            pltpu.SemaphoreType.DMA,
            pltpu.SemaphoreType.DMA,
            pltpu.SemaphoreType.DMA,
            pltpu.SemaphoreType.DMA,
            pltpu.SemaphoreType.REGULAR,
        ],
        compiler_params=pltpu.CompilerParams(
            collective_id=0, has_side_effects=True, vmem_limit_bytes=24 * 2**20
        ),
    )(*stored, grad)
    return pl.pallas_call(
        adamw,
        name="adamw",
        out_shape=(shape, shape, shape),
        in_specs=[vmem] * 3,
        out_specs=(hbm, hbm, hbm),
        scratch_shapes=[
            pltpu.VMEM((3, MATS, BLOCK, 768), jnp.float32),
            pltpu.SemaphoreType.DMA,
        ],
        compiler_params=pltpu.CompilerParams(vmem_limit_bytes=24 * 2**20),
    )(wide, gv, total)


def solution(mesh):
    placed = (
        P(None, ("dp", "tensor"), None),
        P(None, ("dp", "tensor"), None),
        P(None, ("dp", "tensor"), None),
        P(None, "dp", "tensor"),
    )
    return jax.shard_map(
        local,
        mesh=mesh,
        in_specs=placed,
        out_specs=(P(None, "dp", "tensor"), P(None, "dp", "tensor"), P(None, "dp", "tensor")),
        check_vma=False,
    )
```

time: 105 us -> 88.1 us (0.84)
  Pallas kernels: 96.3 us -> 86.4 us
  local copies, waits for them, and re-layouts: 7.63 us -> 0 us
    pallas_call x1 -> x2, Pallas kernels: 96.3 us -> 86.4 us  [the longest x1 84.7 us: local(): pl.pallas_call(regroup, name='regroup', out_shape=(pltpu.VMEM((6, MATS, 1...]
    unnamed x11 -> x0, local copies, waits for them, and re-layouts: 7.63 us -> none
where the time goes in v2:
time: 88.1 us; the launch traced here: 87.1 us
  Pallas kernels  86.4 us (98%)
    pallas_call x1, Pallas kernels, local(): pl.pallas_call(regroup, name='regroup', out_shape=(pltpu.VMEM((6, MATS, 1...  84.7 us

profile of v2, /device:TPU:65, one launch (start us, length us, event | category | flops | bytes accessed | tf_op | source)
XLA Modules:
  0.0 87.1 jit_solution(257098256761814556)
XLA Ops:
  0.6 84.7 %regroup.1 = (f32[6,8,128,128]{3,2,1,0:T(8,128)S(1)}, f32[8,40,768]{2,1,0:T(8,128)S(1)}, f32[1,128]{1,0:T(1,128)S(1)}) custom-call(f32[6,8,5120]{2,1,0:T(8,128)} %bitcast.3, f32[6,8,5120]{2,1,0:T(8,128)} %bitcast.4, f32[6,8,5120]{2,1,0:T(8,128)} %bitcast.5, f32[8,40,768]{2,1,0:T(8,128)} %g_hbm.1), custom_call_target="tpu_custom_call" | custom-call | tf_op jit(solution)/shard_map/regroup/pallas_call | solution.py:221
  85.4 1.7 %adamw.1 = (f32[8,40,768]{2,1,0:T(8,128)}, f32[8,40,768]{2,1,0:T(8,128)}, f32[8,40,768]{2,1,0:T(8,128)}) custom-call(f32[6,8,128,128]{3,2,1,0:T(8,128)S(1)} %get-tuple-element.6.wide, f32[8,40,768]{2,1,0:T(8,128)S(1)} %get-tuple-element.7.gv, f32[1,128]{1,0:T(1,128)S(1)} %get-tuple-element.8.total), custom_call_target="tpu_custom_call" | custom-call | tf_op jit(solution)/shard_map/adamw/pallas_call | solution.py:253

commit v3 on v2

--- a/solution.py
+++ b/solution.py
@@ -19,32 +19,57 @@
 
 def pack_group(xin, src, zt):
     lane = lax.broadcasted_iota(jnp.int32, (8, 128), 1)
+    row = lax.broadcasted_iota(jnp.int32, (8, 128), 0)
+    low = row < 3
+    off1 = jnp.where(low, 80, 72)
+    off2 = jnp.where(low, 120, jnp.where(row == 3, 104, 88))
     base = pl.multiple_of(zt * 640, 128)
+
+    def load(a, h, t):
+        return xin[a, h, :, pl.ds(base + 128 * t, 128)]
+
     for h in range(ROWS):
-        tiles = []
-        for a in range(3):
-            row = []
+        tiles = [
+            [load(a, h, t) if a == 0 else pltpu.roll(load(a, h, t), 40 * a, 1) for t in range(5)]
+            for a in range(3)
+        ]
+        if h < 5:
+            extra = [pltpu.roll(load(2, 5, t), 120 - 8 * h, 1) for t in range(5)]
+        else:
+            fill1, fill2 = [], []
             for t in range(5):
-                v = xin[a, h, :, pl.ds(base + 128 * t, 128)]
-                row.append(v if a == 0 else pltpu.roll(v, 40 * a, 1))
-            tiles.append(row)
+                x, y = load(0, 5, t), load(1, 5, t)
+                up = [pltpu.roll(pltpu.roll(y, 8 - d, 0), k, 1) for d, k in ((5, 120), (2, 72), (4, 104), (3, 88))]
+                fill1.append(jnp.where(low, pltpu.roll(pltpu.roll(x, 3, 0), 80, 1), up[1]))
+                fill2.append(jnp.where(low, up[0], jnp.where(row == 3, up[2], up[3])))
         for p in range(16):
             start = (40 * p) % 128
             t0 = (40 * p) // 128
             u = (lane + (128 - start)) & 127
-            pieces = []
-            for a in range(3):
-                piece = tiles[a][t0]
-                if start + 40 > 128:
-                    piece = jnp.where(u < 40 * a + 128 - start, piece, tiles[a][t0 + 1])
-                pieces.append(piece)
-            out = jnp.where(u < 40, pieces[0], jnp.where(u < 80, pieces[1], pieces[2]))
-            src[zt * 16 + p, 8 * h : 8 * h + 8, :] = out
+            split = start + 40 > 128
+
+            def pick(v, offset):
+                if not split:
+                    return v[t0]
+                return jnp.where(u - offset < 128 - start, v[t0], v[t0 + 1])
+
+            first, second = pick(tiles[0], 0), pick(tiles[1], 40)
+            if h < 5:
+                third = pick(tiles[2], 80)
+                out = jnp.where(u < 40, first, jnp.where(u < 80, second, third))
+                src[zt * 16 + p, 8 * h : 8 * h + 8, :] = jnp.where(
+                    u < 120, out, extra[(5 * p + h) // 16]
+                )
+            else:
+                last = jnp.logical_or(u >= 120, jnp.logical_and(u >= 112, row >= 3))
+                third = jnp.where(last, pick(fill2, off2), pick(fill1, off1))
+                out = jnp.where(u < 40, first, jnp.where(u < 80, second, third))
+                src[zt * 16 + p, 40:45, :] = out[0:5]
 
 
 def regroup(
-    x0, x1, x2, g_hbm, wide, gv, total,
-    xin, src, arr, mine_sum, plane_sums, col_sums, sib_sum,
+    x0, x1, x2, g_hbm, arr, gv, total,
+    xin, src, mine_sum, plane_sums, col_sums, sib_sum,
     in_sem, g_sem, send_sem, recv_sem, small_send, plane_recv, col_recv, sib_recv, col_sem,
 ):
     s = lax.axis_index("dp")
@@ -89,7 +114,7 @@
     lax.fori_loop(4, 8, pack, 0)
     pl.semaphore_wait(col_sem, 7)
 
-    slot = arr.at[pl.ds(pl.multiple_of(48 * dl, 8), 48)]
+    slot = arr.at[pl.ds(pl.multiple_of(48 * dl, 8), 45)]
 
     def send(j, carry):
         for e in range(8):
@@ -161,15 +186,7 @@
     swap.wait()
     total[...] = part + sib_sum[0]
 
-    pltpu.make_async_copy(arr, arr, recv_sem).wait()
-
-    def flip(m, carry):
-        for t in range(6):
-            wide[t, m] = arr[pl.ds(t * 1024 + m, 128, 8), :].T
-        return carry
-
-    lax.fori_loop(0, MATS, flip, 0)
-
+    pltpu.make_async_copy(src, src, recv_sem).wait()
     sent = src.at[pl.ds(0, 127)]
     pltpu.make_async_copy(sent, sent, send_sem).wait()
 
@@ -178,21 +195,39 @@
         pltpu.make_async_copy(src.at[127], src.at[127], send_sem).wait()
 
 
-def adamw(wide, gv, total, o0, o1, o2, outv, out_sem):
+def adamw(arr, gv, total, o0, o1, o2, wide, outv, out_sem):
     plane = lax.axis_index("dp") % 16
     limit = 0.5 * jnp.sqrt(jnp.float32(COUNT))
     scale = jnp.minimum(1.0, limit / (jnp.sqrt(total[...]) + 1e-06))
     scale = jnp.broadcast_to(scale, (8, 128))
-
-    def update(m, carry):
+    lane = lax.broadcasted_iota(jnp.int32, (8, 128), 1)
+    sixth = [(lane + 128 * t) % 6 == 5 for t in range(3)]
+
+    def slot(t, m, j):
+        return wide[t, m, pl.ds(pl.multiple_of(8 * ((5 * plane + j) % 16), 8), 8), :]
+
+    def update(m, late):
+        for t in range(6):
+            wide[t, m] = arr[pl.ds(t * 1024 + m, 128, 8), :].T
+        spare = [slot(t, m, 15) for t in range(6)]
         for w in range(5):
-            spots = [pl.multiple_of(8 * ((5 * plane + 5 * a + w) % 16), 8) for a in range(3)]
+            moved = [pltpu.roll(v, 5 - w, 1) for v in spare]
             for t in range(6):
                 rows = slice(8 * w, 8 * w + 8)
                 cols = slice(128 * t, 128 * t + 128)
-                weights = wide[t, m, pl.ds(spots[0], 8), :]
-                first = wide[t, m, pl.ds(spots[1], 8), :]
-                second = wide[t, m, pl.ds(spots[2], 8), :]
+                weights = slot(t, m, w)
+                first = slot(t, m, 5 + w)
+                back = moved[t] if t % 3 == 0 else jnp.where(lane < 5 - w, moved[t - 1], moved[t])
+                second = jnp.where(sixth[t % 3], back, slot(t, m, 10 + w))
+                if late:
+                    weights = jnp.where(sixth[t % 3], slot(t, m - 5, 10 + w), weights)
+                    if w == 0:
+                        other = slot(t, m - 5, 15)
+                    elif m < 7:
+                        other = slot(t, m - 2, 9 + w)
+                    else:
+                        other = slot(t, 3 + (w - 1) // 2, 14 + (w - 1) % 2)
+                    first = jnp.where(sixth[t % 3], other, first)
                 clipped = scale * gv[m, rows, cols]
                 new_first = 0.9 * first + 0.1 * clipped
                 new_second = 0.95 * second + 0.05 * clipped * clipped
@@ -202,9 +237,14 @@
                 outv[2, m, rows, cols] = new_second
         for a, o in enumerate((o0, o1, o2)):
             pltpu.make_async_copy(outv.at[a, m], o.at[m], out_sem).start()
+
+    def early(m, carry):
+        update(m, False)
         return carry
 
-    lax.fori_loop(0, MATS, update, 0)
+    lax.fori_loop(0, 5, early, 0)
+    for m in range(5, MATS):
+        update(m, True)
     for a, o in enumerate((o0, o1, o2)):
         pltpu.make_async_copy(outv.at[a], o, out_sem).wait()
 
@@ -218,11 +258,11 @@
         for x in (master, moment_one, moment_two)
     ]
     grad = pltpu.with_memory_space_constraint(grad, pltpu.HBM)
-    wide, gv, total = pl.pallas_call(
+    arrived, gv, total = pl.pallas_call(
         regroup,
         name="regroup",
         out_shape=(
-            pltpu.VMEM((6, MATS, 128, 128), jnp.float32),
+            pltpu.VMEM((128 * 48, 128), jnp.float32),
             pltpu.VMEM(grad.shape, jnp.float32),
             pltpu.VMEM((1, 128), jnp.float32),
         ),
@@ -230,8 +270,7 @@
         out_specs=(vmem, vmem, vmem),
         scratch_shapes=[
             pltpu.VMEM((3, ROWS, MATS, D), jnp.float32),
-            pltpu.VMEM((128, 48, 128), jnp.float32),
-            pltpu.VMEM((128 * 48, 128), jnp.float32),
+            pltpu.VMEM((128, 45, 128), jnp.float32),
             pltpu.VMEM((1, 1, 128), jnp.float32),
             pltpu.VMEM((16, 1, 128), jnp.float32),
             pltpu.VMEM((8, 1, 128), jnp.float32),
@@ -257,11 +296,12 @@
         in_specs=[vmem] * 3,
         out_specs=(hbm, hbm, hbm),
         scratch_shapes=[
+            pltpu.VMEM((6, MATS, 128, 128), jnp.float32),
             pltpu.VMEM((3, MATS, BLOCK, 768), jnp.float32),
             pltpu.SemaphoreType.DMA,
         ],
         compiler_params=pltpu.CompilerParams(vmem_limit_bytes=24 * 2**20),
-    )(wide, gv, total)
+    )(arrived, gv, total)
 
 
 def solution(mesh):

time: 88.1 us -> 84.1 us (0.955)
  Pallas kernels: 86.4 us -> 82.5 us
    pallas_call x1, Pallas kernels: 84.7 us -> 79.2 us  [local(): pl.pallas_call(regroup, name='regroup', out_shape=(pltpu.VMEM((128 * 48,...]
    pallas_call x1, Pallas kernels: 1.71 us -> 3.33 us  [local(): pl.pallas_call(adamw, name='adamw', out_shape=(shape, shape, shape), in_s...]
where the time goes in v3:
time: 84.1 us; the launch traced here: 83.1 us
  Pallas kernels  82.5 us (98%)
    pallas_call x1, Pallas kernels, local(): pl.pallas_call(regroup, name='regroup', out_shape=(pltpu.VMEM((128 * 48,...  79.2 us
    pallas_call x1, Pallas kernels, local(): pl.pallas_call(adamw, name='adamw', out_shape=(shape, shape, shape), in_s...  3.33 us

profile of v3, /device:TPU:65, one launch (start us, length us, event | category | flops | bytes accessed | tf_op | source)
XLA Modules:
  0.0 83.1 jit_solution(15429613340196537955)
XLA Ops:
  0.6 79.2 %regroup.1 = (f32[6144,128]{1,0:T(8,128)S(1)}, f32[8,40,768]{2,1,0:T(8,128)S(1)}, f32[1,128]{1,0:T(1,128)S(1)}) custom-call(f32[6,8,5120]{2,1,0:T(8,128)} %bitcast.3, f32[6,8,5120]{2,1,0:T(8,128)} %bitcast.4, f32[6,8,5120]{2,1,0:T(8,128)} %bitcast.5, f32[8,40,768]{2,1,0:T(8,128)} %g_hbm.1), custom_call_target="tpu_custom_call" | custom-call | tf_op jit(solution)/shard_map/regroup/pallas_call | solution.py:261
  79.8 3.3 %adamw.1 = (f32[8,40,768]{2,1,0:T(8,128)}, f32[8,40,768]{2,1,0:T(8,128)}, f32[8,40,768]{2,1,0:T(8,128)}) custom-call(f32[6144,128]{1,0:T(8,128)S(1)} %get-tuple-element.6.arr, f32[8,40,768]{2,1,0:T(8,128)S(1)} %get-tuple-element.7.gv, f32[1,128]{1,0:T(1,128)S(1)} %get-tuple-element.8.total), custom_call_target="tpu_custom_call" | custom-call | tf_op jit(solution)/shard_map/adamw/pallas_call | solution.py:292

commit v4 on v3

--- a/solution.py
+++ b/solution.py
@@ -67,11 +67,55 @@
                 src[zt * 16 + p, 40:45, :] = out[0:5]
 
 
+def flip(arr, wide, grp, m):
+    for t in range(3):
+        start = pl.multiple_of(grp * 3072, 8) + t * 1024 + m
+        wide[m][t] = arr[pl.ds(start, 128, 8), :].T
+
+
+def update(wide, gv, scale, grp, m, out):
+    plane = lax.axis_index("dp") % 16
+    lane = lax.broadcasted_iota(jnp.int32, (8, 128), 1)
+    sixth = [(lane + 128 * t) % 6 == 5 for t in range(3)]
+    spots = [pl.multiple_of(8 * ((5 * plane + j) % 16), 8) for j in range(16)]
+
+    def slot(t, mat, j):
+        return wide[mat][t, pl.ds(spots[j], 8), :]
+
+    spare = [slot(t, m, 15) for t in range(3)]
+    for w in range(5):
+        moved = [pltpu.roll(v, 5 - w, 1) for v in spare]
+        for t in range(3):
+            rows = slice(8 * w, 8 * w + 8)
+            cols = slice(128 * t, 128 * t + 128)
+            weights = slot(t, m, w)
+            first = slot(t, m, 5 + w)
+            back = moved[t] if t == 0 else jnp.where(lane < 5 - w, moved[t - 1], moved[t])
+            second = jnp.where(sixth[t], back, slot(t, m, 10 + w))
+            if m >= 5:
+                weights = jnp.where(sixth[t], slot(t, m - 5, 10 + w), weights)
+                if w == 0:
+                    other = slot(t, m - 5, 15)
+                elif m < 7:
+                    other = slot(t, m - 2, 9 + w)
+                else:
+                    other = slot(t, 3 + (w - 1) // 2, 14 + (w - 1) % 2)
+                first = jnp.where(sixth[t], other, first)
+            clipped = scale * gv[m, rows, pl.ds(pl.multiple_of(grp * 384, 128) + 128 * t, 128)]
+            new_first = 0.9 * first + 0.1 * clipped
+            new_second = 0.95 * second + 0.05 * clipped * clipped
+            step = new_first / bias_first / (jnp.sqrt(new_second / bias_second) + 1e-08)
+            out(0, rows, cols, weights * (1.0 - 0.05 * 0.1) - 0.05 * step)
+            out(1, rows, cols, new_first)
+            out(2, rows, cols, new_second)
+
+
 def regroup(
-    x0, x1, x2, g_hbm, arr, gv, total,
-    xin, src, mine_sum, plane_sums, col_sums, sib_sum,
+    x0, x1, x2, g_hbm, arr, gv, scale_out, early,
+    xin, src, mine_sum, plane_sums, col_sums, sib_sum, w0, w1, w2, w3, w4, w5, w6, w7,
     in_sem, g_sem, send_sem, recv_sem, small_send, plane_recv, col_recv, sib_recv, col_sem,
 ):
+    wide = (w0, w1, w2, w3, w4, w5, w6, w7)
     s = lax.axis_index("dp")
     c = lax.axis_index("tensor")
     z = s // 16
@@ -107,32 +151,44 @@
         pack_group(xin, src, zt)
         return carry
 
-    lax.fori_loop(0, 4, pack, 0)
     pl.semaphore_wait(barrier, 38)
     for i in range(1, 8):
         pl.semaphore_signal(col_sem, inc=1, device_id=(s ^ (16 * i), c), device_id_type=MESH)
-    lax.fori_loop(4, 8, pack, 0)
+    lax.fori_loop(0, 8, pack, 0)
     pl.semaphore_wait(col_sem, 7)
 
     slot = arr.at[pl.ds(pl.multiple_of(48 * dl, 8), 45)]
 
-    def send(j, carry):
-        for e in range(8):
-            t = s ^ (16 * (7 - e)) ^ (j ^ (2 * e))
-            message = pltpu.make_async_remote_copy(
-                src_ref=src.at[t],
-                dst_ref=slot,
-                send_sem=send_sem,
-                recv_sem=recv_sem,
-                device_id=(t, half),
-                device_id_type=MESH,
-            )
-            if e < 7:
-                message.start()
-            else:
-                own = jnp.logical_and(j == 14, mine)
-                pl.when(jnp.logical_not(own))(message.start)
-                pl.when(own)(pltpu.make_async_copy(src.at[t], slot, recv_sem).start)
+    def send(offsets, r, j, sem):
+        kz = offsets[r]
+        t = s ^ (16 * kz) ^ (j ^ (4 * r))
+        message = pltpu.make_async_remote_copy(
+            src_ref=src.at[t],
+            dst_ref=slot,
+            send_sem=send_sem,
+            recv_sem=sem,
+            device_id=(t, half),
+            device_id_type=MESH,
+        )
+        if kz > 0:
+            message.start()
+        else:
+            own = jnp.logical_and(j == 4 * r, mine)
+            pl.when(jnp.logical_not(own))(message.start)
+            pl.when(own)(pltpu.make_async_copy(src.at[t], slot, sem).start)
+
+    def first_phase(j, carry):
+        for r in range(4):
+            send((7, 2, 6, 3), r, j, recv_sem.at[0])
+        return carry
+
+    lates = [4 * jnp.minimum(z ^ kz, 4) for kz in (4, 1, 5, 0)]
+
+    def second_phase(q, carry):
+        for r in range(4):
+            j = q - lates[r]
+            inside = jnp.logical_and(j >= 0, j < 16)
+            pl.when(inside)(lambda: send((4, 1, 5, 0), r, j, recv_sem.at[1]))
         return carry
 
     def small(dst, recv, peer, core):
@@ -145,7 +201,7 @@
             device_id_type=MESH,
         )
 
-    lax.fori_loop(0, 2, send, 0)
+    lax.fori_loop(0, 4, first_phase, 0)
 
     gcopy.wait()
 
@@ -163,7 +219,7 @@
     plane_out = [small(plane_sums.at[pl.ds(plane, 1)], plane_recv, s ^ i, c) for i in range(1, 16)]
     for copy in plane_out:
         copy.start()
-    lax.fori_loop(2, 8, send, 0)
+    lax.fori_loop(4, 16, first_phase, 0)
     for copy in plane_out:
         copy.wait_send()
     first15 = plane_sums.at[pl.ds(0, 15)]
@@ -174,7 +230,7 @@
     col_out = [small(col_sums.at[pl.ds(z, 1)], col_recv, s ^ (16 * i), c) for i in range(1, 8)]
     for copy in col_out:
         copy.start()
-    lax.fori_loop(8, 16, send, 0)
+    lax.fori_loop(0, 32, second_phase, 0)
     for copy in col_out:
         copy.wait_send()
     first7 = col_sums.at[pl.ds(0, 7)]
@@ -184,9 +240,23 @@
     swap = small(sib_sum, sib_recv, s, 1 - c)
     swap.start()
     swap.wait()
-    total[...] = part + sib_sum[0]
-
-    pltpu.make_async_copy(src, src, recv_sem).wait()
+    limit = 0.5 * jnp.sqrt(jnp.float32(COUNT))
+    scale = jnp.minimum(1.0, limit / (jnp.sqrt(part + sib_sum[0]) + 1e-06))
+    scale = jnp.broadcast_to(scale, (8, 128))
+    scale_out[...] = scale
+
+    some = src.at[pl.ds(0, 64)]
+    pltpu.make_async_copy(some, some, recv_sem.at[0]).wait()
+    grp = 1 - (z // 2) % 2
+    for m in range(MATS):
+        flip(arr, wide, grp, m)
+
+        def keep(a, rows, cols, value):
+            early[a, m, rows, cols] = value
+
+        update(wide, gv, scale, grp, m, keep)
+
+    pltpu.make_async_copy(some, some, recv_sem.at[1]).wait()
     sent = src.at[pl.ds(0, 127)]
     pltpu.make_async_copy(sent, sent, send_sem).wait()
 
@@ -195,58 +265,39 @@
         pltpu.make_async_copy(src.at[127], src.at[127], send_sem).wait()
 
 
-def adamw(arr, gv, total, o0, o1, o2, wide, outv, out_sem):
-    plane = lax.axis_index("dp") % 16
-    limit = 0.5 * jnp.sqrt(jnp.float32(COUNT))
-    scale = jnp.minimum(1.0, limit / (jnp.sqrt(total[...]) + 1e-06))
-    scale = jnp.broadcast_to(scale, (8, 128))
-    lane = lax.broadcasted_iota(jnp.int32, (8, 128), 1)
-    sixth = [(lane + 128 * t) % 6 == 5 for t in range(3)]
-
-    def slot(t, m, j):
-        return wide[t, m, pl.ds(pl.multiple_of(8 * ((5 * plane + j) % 16), 8), 8), :]
-
-    def update(m, late):
-        for t in range(6):
-            wide[t, m] = arr[pl.ds(t * 1024 + m, 128, 8), :].T
-        spare = [slot(t, m, 15) for t in range(6)]
-        for w in range(5):
-            moved = [pltpu.roll(v, 5 - w, 1) for v in spare]
-            for t in range(6):
-                rows = slice(8 * w, 8 * w + 8)
-                cols = slice(128 * t, 128 * t + 128)
-                weights = slot(t, m, w)
-                first = slot(t, m, 5 + w)
-                back = moved[t] if t % 3 == 0 else jnp.where(lane < 5 - w, moved[t - 1], moved[t])
-                second = jnp.where(sixth[t % 3], back, slot(t, m, 10 + w))
-                if late:
-                    weights = jnp.where(sixth[t % 3], slot(t, m - 5, 10 + w), weights)
-                    if w == 0:
-                        other = slot(t, m - 5, 15)
-                    elif m < 7:
-                        other = slot(t, m - 2, 9 + w)
-                    else:
-                        other = slot(t, 3 + (w - 1) // 2, 14 + (w - 1) % 2)
-                    first = jnp.where(sixth[t % 3], other, first)
-                clipped = scale * gv[m, rows, cols]
-                new_first = 0.9 * first + 0.1 * clipped
-                new_second = 0.95 * second + 0.05 * clipped * clipped
-                step = new_first / bias_first / (jnp.sqrt(new_second / bias_second) + 1e-08)
-                outv[0, m, rows, cols] = weights * (1.0 - 0.05 * 0.1) - 0.05 * step
-                outv[1, m, rows, cols] = new_first
-                outv[2, m, rows, cols] = new_second
-        for a, o in enumerate((o0, o1, o2)):
-            pltpu.make_async_copy(outv.at[a, m], o.at[m], out_sem).start()
-
-    def early(m, carry):
-        update(m, False)
-        return carry
-
-    lax.fori_loop(0, 5, early, 0)
-    for m in range(5, MATS):
-        update(m, True)
-    for a, o in enumerate((o0, o1, o2)):
-        pltpu.make_async_copy(outv.at[a], o, out_sem).wait()
+def adamw(
+    arr, gv, scale_in, early, o0, o1, o2,
+    late, w0, w1, w2, w3, w4, w5, w6, w7, early_sem, late_sem,
+):
+    wide = (w0, w1, w2, w3, w4, w5, w6, w7)
+    grp = (lax.axis_index("dp") // 32) % 2
+    there = pl.ds(pl.multiple_of(384 * (1 - grp), 128), 384)
+    here = pl.ds(pl.multiple_of(384 * grp, 128), 384)
+    outs = (o0, o1, o2)
+    early_out = [
+        pltpu.make_async_copy(early.at[a, m], o.at[m, :, there], early_sem)
+        for m in range(MATS)
+        for a, o in enumerate(outs)
+    ]
+    for copy in early_out:
+        copy.start()
+    scale = scale_in[...]
+    late_out = []
+    flip(arr, wide, grp, 0)
+    for m in range(MATS):
+        if m + 1 < MATS:
+            flip(arr, wide, grp, m + 1)
+
+        def keep(a, rows, cols, value):
+            late[a, m, rows, cols] = value
+
+        update(wide, gv, scale, grp, m, keep)
+        for a, o in enumerate(outs):
+            late_out.append(pltpu.make_async_copy(late.at[a, m], o.at[m, :, here], late_sem))
+            late_out[-1].start()
+    for a in range(3):
+        pltpu.make_async_copy(early.at[a], early.at[a], early_sem).wait()
+        pltpu.make_async_copy(late.at[a], late.at[a], late_sem).wait()
 
 
 def local(master, moment_one, moment_two, grad):
@@ -258,16 +309,19 @@
         for x in (master, moment_one, moment_two)
     ]
     grad = pltpu.with_memory_space_constraint(grad, pltpu.HBM)
-    arrived, gv, total = pl.pallas_call(
+    wide = [pltpu.VMEM((3, 128, 128), jnp.float32)] * MATS
+    half = (3, MATS, BLOCK, 384)
+    arrived, gv, scale, early = pl.pallas_call(
         regroup,
         name="regroup",
         out_shape=(
             pltpu.VMEM((128 * 48, 128), jnp.float32),
             pltpu.VMEM(grad.shape, jnp.float32),
-            pltpu.VMEM((1, 128), jnp.float32),
+            pltpu.VMEM((8, 128), jnp.float32),
+            pltpu.VMEM(half, jnp.float32),
         ),
         in_specs=[hbm] * 4,
-        out_specs=(vmem, vmem, vmem),
+        out_specs=(vmem, vmem, vmem, vmem),
         scratch_shapes=[
             pltpu.VMEM((3, ROWS, MATS, D), jnp.float32),
             pltpu.VMEM((128, 45, 128), jnp.float32),
@@ -275,10 +329,11 @@
             pltpu.VMEM((16, 1, 128), jnp.float32),
             pltpu.VMEM((8, 1, 128), jnp.float32),
             pltpu.VMEM((1, 1, 128), jnp.float32),
+            *wide,
             pltpu.SemaphoreType.DMA((8,)),
             pltpu.SemaphoreType.DMA,
             pltpu.SemaphoreType.DMA,
-            pltpu.SemaphoreType.DMA,
+            pltpu.SemaphoreType.DMA((2,)),
             pltpu.SemaphoreType.DMA,
             pltpu.SemaphoreType.DMA,
             pltpu.SemaphoreType.DMA,
@@ -293,15 +348,16 @@
         adamw,
         name="adamw",
         out_shape=(shape, shape, shape),
-        in_specs=[vmem] * 3,
+        in_specs=[vmem] * 4,
         out_specs=(hbm, hbm, hbm),
         scratch_shapes=[
-            pltpu.VMEM((6, MATS, 128, 128), jnp.float32),
-            pltpu.VMEM((3, MATS, BLOCK, 768), jnp.float32),
+            pltpu.VMEM(half, jnp.float32),
+            *wide,
+            pltpu.SemaphoreType.DMA,
             pltpu.SemaphoreType.DMA,
         ],
         compiler_params=pltpu.CompilerParams(vmem_limit_bytes=24 * 2**20),
-    )(arrived, gv, total)
+    )(arrived, gv, scale, early)
 
 
 def solution(mesh):

time: 84.1 us -> 81.9 us (0.974)
  Pallas kernels: 82.5 us -> 80.3 us
    pallas_call x1, Pallas kernels: 79.2 us -> 78 us  [local(): pl.pallas_call(regroup, name='regroup', out_shape=(pltpu.VMEM((128 * 48,...]
    pallas_call x1, Pallas kernels: 3.33 us -> 2.23 us  [local(): pl.pallas_call(adamw, name='adamw', out_shape=(shape, shape, shape), in_s...]
where the time goes in v4:
time: 81.9 us; the launch traced here: 80.9 us
  Pallas kernels  80.3 us (98%)
    pallas_call x1, Pallas kernels, local(): pl.pallas_call(regroup, name='regroup', out_shape=(pltpu.VMEM((128 * 48,...  78 us
    pallas_call x1, Pallas kernels, local(): pl.pallas_call(adamw, name='adamw', out_shape=(shape, shape, shape), in_s...  2.23 us

profile of v4, /device:TPU:65, one launch (start us, length us, event | category | flops | bytes accessed | tf_op | source)
XLA Modules:
  0.0 80.9 jit_solution(15596053826597004058)
XLA Ops:
  0.6 78.0 %regroup.1 = (f32[6144,128]{1,0:T(8,128)S(1)}, f32[8,40,768]{2,1,0:T(8,128)S(1)}, f32[8,128]{1,0:T(8,128)S(1)}, f32[3,8,40,384]{3,2,1,0:T(8,128)S(1)}) custom-call(f32[6,8,5120]{2,1,0:T(8,128)} %bitcast.3, f32[6,8,5120]{2,1,0:T(8,128)} %bitcast.4, f32[6,8,5120]{2,1,0:T(8,128)} %bitcast.5, f32[8,40,768]{2,1,0:T(8,128)} %g_hbm.1), custom_call_target="tpu_custom_call" | custom-call | tf_op jit(solution)/shard_map/regroup/pallas_call | solution.py:314
  78.7 2.2 %adamw.1 = (f32[8,40,768]{2,1,0:T(8,128)}, f32[8,40,768]{2,1,0:T(8,128)}, f32[8,40,768]{2,1,0:T(8,128)}) custom-call(f32[6144,128]{1,0:T(8,128)S(1)} %get-tuple-element.7.arr, f32[8,40,768]{2,1,0:T(8,128)S(1)} %get-tuple-element.8.gv, f32[8,128]{1,0:T(8,128)S(1)} %get-tuple-element.9.scale_in, f32[3,8,40,384]{3,2,1,0:T(8,128)S(1)} %get-tuple-element.10.early), custom_call_target="tpu_custom_call" | custom-call | tf_op jit(solution)/shard_map/adamw/pallas_call | solution.py:347

commit v5 on v4

--- a/solution.py
+++ b/solution.py
@@ -15,6 +15,12 @@
 bias_first = 0.9999734386011124
 bias_second = 0.994079470779666
 COUNT = float(MATS * D * MOE_FF)
+
+
+FIRST = (7, 6, 2, 3)
+BEGIN = {7: 0, 6: 0, 2: 8, 3: 8, 4: 16, 5: 16, 1: 24, 0: 24}
+SKEW = {7: 0, 2: 1, 6: 2, 3: 3, 4: 0, 1: 1, 5: 2, 0: 3}
+LATER = (2, 2)
 
 
 def pack_group(xin, src, zt):
@@ -159,36 +165,30 @@
 
     slot = arr.at[pl.ds(pl.multiple_of(48 * dl, 8), 45)]
 
-    def send(offsets, r, j, sem):
-        kz = offsets[r]
-        t = s ^ (16 * kz) ^ (j ^ (4 * r))
-        message = pltpu.make_async_remote_copy(
-            src_ref=src.at[t],
-            dst_ref=slot,
-            send_sem=send_sem,
-            recv_sem=sem,
-            device_id=(t, half),
-            device_id_type=MESH,
-        )
-        if kz > 0:
-            message.start()
-        else:
-            own = jnp.logical_and(j == 4 * r, mine)
-            pl.when(jnp.logical_not(own))(message.start)
-            pl.when(own)(pltpu.make_async_copy(src.at[t], slot, sem).start)
-
-    def first_phase(j, carry):
-        for r in range(4):
-            send((7, 2, 6, 3), r, j, recv_sem.at[0])
-        return carry
-
-    lates = [4 * jnp.minimum(z ^ kz, 4) for kz in (4, 1, 5, 0)]
-
-    def second_phase(q, carry):
-        for r in range(4):
-            j = q - lates[r]
+    begins = {}
+    for kz, begin in BEGIN.items():
+        begins[kz] = begin if kz in FIRST else begin + LATER[kz // 4] * jnp.minimum(z ^ kz, 4)
+
+    def turn(q, carry):
+        for kz, r in SKEW.items():
+            j = q - begins[kz]
+            t = s ^ (16 * kz) ^ (j ^ (4 * r))
+            sem = recv_sem.at[0 if kz in FIRST else 1]
+            message = pltpu.make_async_remote_copy(
+                src_ref=src.at[t],
+                dst_ref=slot,
+                send_sem=send_sem,
+                recv_sem=sem,
+                device_id=(t, half),
+                device_id_type=MESH,
+            )
             inside = jnp.logical_and(j >= 0, j < 16)
-            pl.when(inside)(lambda: send((4, 1, 5, 0), r, j, recv_sem.at[1]))
+            if kz > 0:
+                pl.when(inside)(message.start)
+            else:
+                own = jnp.logical_and(j == 4 * r, mine)
+                pl.when(jnp.logical_and(inside, jnp.logical_not(own)))(message.start)
+                pl.when(own)(pltpu.make_async_copy(src.at[t], slot, sem).start)
         return carry
 
     def small(dst, recv, peer, core):
@@ -201,7 +201,7 @@
             device_id_type=MESH,
         )
 
-    lax.fori_loop(0, 4, first_phase, 0)
+    lax.fori_loop(0, 4, turn, 0)
 
     gcopy.wait()
 
@@ -219,7 +219,7 @@
     plane_out = [small(plane_sums.at[pl.ds(plane, 1)], plane_recv, s ^ i, c) for i in range(1, 16)]
     for copy in plane_out:
         copy.start()
-    lax.fori_loop(4, 16, first_phase, 0)
+    lax.fori_loop(4, 12, turn, 0)
     for copy in plane_out:
         copy.wait_send()
     first15 = plane_sums.at[pl.ds(0, 15)]
@@ -230,7 +230,7 @@
     col_out = [small(col_sums.at[pl.ds(z, 1)], col_recv, s ^ (16 * i), c) for i in range(1, 8)]
     for copy in col_out:
         copy.start()
-    lax.fori_loop(0, 32, second_phase, 0)
+    lax.fori_loop(12, 48, turn, 0)
     for copy in col_out:
         copy.wait_send()
     first7 = col_sums.at[pl.ds(0, 7)]

time: 81.9 us -> 81.5 us (level); the launches traced: 80.9 us -> 81.3 us
  no operation moved by 1% of the time
where the time goes in v5:
time: 81.5 us; the launch traced here: 81.3 us
  Pallas kernels  80.7 us (99%)
    pallas_call x1, Pallas kernels, local(): pl.pallas_call(regroup, name='regroup', out_shape=(pltpu.VMEM((128 * 48,...  78.5 us
    pallas_call x1, Pallas kernels, local(): pl.pallas_call(adamw, name='adamw', out_shape=(shape, shape, shape), in_s...  2.23 us

profile of v5, /device:TPU:65, one launch (start us, length us, event | category | flops | bytes accessed | tf_op | source)
XLA Modules:
  0.0 81.3 jit_solution(13447145805390661021)
XLA Ops:
  0.6 78.5 %regroup.1 = (f32[6144,128]{1,0:T(8,128)S(1)}, f32[8,40,768]{2,1,0:T(8,128)S(1)}, f32[8,128]{1,0:T(8,128)S(1)}, f32[3,8,40,384]{3,2,1,0:T(8,128)S(1)}) custom-call(f32[6,8,5120]{2,1,0:T(8,128)} %bitcast.3, f32[6,8,5120]{2,1,0:T(8,128)} %bitcast.4, f32[6,8,5120]{2,1,0:T(8,128)} %bitcast.5, f32[8,40,768]{2,1,0:T(8,128)} %g_hbm.1), custom_call_target="tpu_custom_call" | custom-call | tf_op jit(solution)/shard_map/regroup/pallas_call | solution.py:314
  79.1 2.2 %adamw.1 = (f32[8,40,768]{2,1,0:T(8,128)}, f32[8,40,768]{2,1,0:T(8,128)}, f32[8,40,768]{2,1,0:T(8,128)}) custom-call(f32[6144,128]{1,0:T(8,128)S(1)} %get-tuple-element.7.arr, f32[8,40,768]{2,1,0:T(8,128)S(1)} %get-tuple-element.8.gv, f32[8,128]{1,0:T(8,128)S(1)} %get-tuple-element.9.scale_in, f32[3,8,40,384]{3,2,1,0:T(8,128)S(1)} %get-tuple-element.10.early), custom_call_target="tpu_custom_call" | custom-call | tf_op jit(solution)/shard_map/adamw/pallas_call | solution.py:347

commit v6 on v5

--- a/solution.py
+++ b/solution.py
@@ -201,7 +201,7 @@
             device_id_type=MESH,
         )
 
-    lax.fori_loop(0, 4, turn, 0)
+    lax.fori_loop(0, 8, turn, 0)
 
     gcopy.wait()
 
@@ -219,7 +219,7 @@
     plane_out = [small(plane_sums.at[pl.ds(plane, 1)], plane_recv, s ^ i, c) for i in range(1, 16)]
     for copy in plane_out:
         copy.start()
-    lax.fori_loop(4, 12, turn, 0)
+    lax.fori_loop(8, 20, turn, 0)
     for copy in plane_out:
         copy.wait_send()
     first15 = plane_sums.at[pl.ds(0, 15)]
@@ -230,7 +230,7 @@
     col_out = [small(col_sums.at[pl.ds(z, 1)], col_recv, s ^ (16 * i), c) for i in range(1, 8)]
     for copy in col_out:
         copy.start()
-    lax.fori_loop(12, 48, turn, 0)
+    lax.fori_loop(20, 48, turn, 0)
     for copy in col_out:
         copy.wait_send()
     first7 = col_sums.at[pl.ds(0, 7)]

time: 81.5 us -> 81.4 us (level)
  no operation moved by 1% of the time
where the time goes in v6:
time: 81.4 us; the launch traced here: 81.2 us
  Pallas kernels  80.6 us (99%)
    pallas_call x1, Pallas kernels, local(): pl.pallas_call(regroup, name='regroup', out_shape=(pltpu.VMEM((128 * 48,...  78.4 us
    pallas_call x1, Pallas kernels, local(): pl.pallas_call(adamw, name='adamw', out_shape=(shape, shape, shape), in_s...  2.23 us

profile of v6, /device:TPU:65, one launch (start us, length us, event | category | flops | bytes accessed | tf_op | source)
XLA Modules:
  0.0 81.2 jit_solution(2517147126544443185)
XLA Ops:
  0.6 78.4 %regroup.1 = (f32[6144,128]{1,0:T(8,128)S(1)}, f32[8,40,768]{2,1,0:T(8,128)S(1)}, f32[8,128]{1,0:T(8,128)S(1)}, f32[3,8,40,384]{3,2,1,0:T(8,128)S(1)}) custom-call(f32[6,8,5120]{2,1,0:T(8,128)} %bitcast.3, f32[6,8,5120]{2,1,0:T(8,128)} %bitcast.4, f32[6,8,5120]{2,1,0:T(8,128)} %bitcast.5, f32[8,40,768]{2,1,0:T(8,128)} %g_hbm.1), custom_call_target="tpu_custom_call" | custom-call | tf_op jit(solution)/shard_map/regroup/pallas_call | solution.py:314
  79.0 2.2 %adamw.1 = (f32[8,40,768]{2,1,0:T(8,128)}, f32[8,40,768]{2,1,0:T(8,128)}, f32[8,40,768]{2,1,0:T(8,128)}) custom-call(f32[6144,128]{1,0:T(8,128)S(1)} %get-tuple-element.7.arr, f32[8,40,768]{2,1,0:T(8,128)S(1)} %get-tuple-element.8.gv, f32[8,128]{1,0:T(8,128)S(1)} %get-tuple-element.9.scale_in, f32[3,8,40,384]{3,2,1,0:T(8,128)S(1)} %get-tuple-element.10.early), custom_call_target="tpu_custom_call" | custom-call | tf_op jit(solution)/shard_map/adamw/pallas_call | solution.py:347
